TPU v7x, 128 devices: a whole 4x4x4 slice. The times are simulated.
128 devices in a mesh: rep: 2 (over z_hi), row: 4 (over x), col: 16 (over z_lo, y, core).
Axes of the slice: x: 4, y: 4, z: 4 (z_hi: 2, z_lo: 2; z = z_hi * 2 + z_lo), core: 2. Of those that a mesh axis runs over, the one named last changes fastest.
Arguments:
- tokens: bfloat16 [2048, 5120], P(('rep', 'col'), 'row'), may hold values from -6 to 6
- grad_out: bfloat16 [2048, 5120], P(('rep', 'col'), 'row'), may hold values from -6 to 6
- gate_weight: bfloat16 [2, 5120, 13824], P('rep', 'row', 'col'), may hold values from -0.078125 to 0.078125
- up_weight: bfloat16 [2, 5120, 13824], P('rep', 'row', 'col'), may hold values from -0.078125 to 0.078125
- down_weight: bfloat16 [2, 13824, 5120], P('rep', 'col', 'row'), may hold values from -0.0546875 to 0.0546875
- gate_buffer: bfloat16 [2, 5120, 13824], P('rep', 'row', 'col'), may hold values from -0.08984375 to 0.08984375
- up_buffer: bfloat16 [2, 5120, 13824], P('rep', 'row', 'col'), may hold values from -0.08984375 to 0.08984375
- down_buffer: bfloat16 [2, 13824, 5120], P('rep', 'col', 'row'), may hold values from -0.08984375 to 0.08984375
Outputs:
- token_grad: bfloat16 [2048, 5120], P(('rep', 'col'), 'row')
- gate_new: bfloat16 [5120, 13824], P('row', 'col')
- up_new: bfloat16 [5120, 13824], P('row', 'col')
- down_new: bfloat16 [13824, 5120], P('col', 'row')
- gate_moment: bfloat16 [5120, 13824], P('row', 'col')
- up_moment: bfloat16 [5120, 13824], P('row', 'col')
- down_moment: bfloat16 [13824, 5120], P('col', 'row')
All inputs are finite; a program needn't handle non-finite values.
Results may differ from a plain program's by a relative error of at most 0.0053.
Values may be sent and summed in bfloat16 or wider, within the bound.
A program may use at most 128 MiB of HBM per device.

v0:
```python
import jax
import jax.numpy as jnp
from jax import lax
from jax.sharding import PartitionSpec as P


def momentum_step(weight, buffer, grad):
    new_buffer = 0.9 * buffer.astype(jnp.float32) + 0.1 * grad
    new_weight = weight.astype(jnp.float32) - 0.5 * (0.3 * grad + 0.7 * new_buffer)
    return (new_weight.astype(jnp.bfloat16), new_buffer.astype(jnp.bfloat16))


def contract_rows(left, right):
    return lax.dot_general(
        left, right, (((0,), (0,)), ((), ())), preferred_element_type=jnp.float32
    )


def contract_cols(left, right):
    return lax.dot_general(
        left, right, (((1,), (1,)), ((), ())), preferred_element_type=jnp.float32
    )


def swiglu_grads(gate, up, back):
    sig = jax.nn.sigmoid(gate)
    active = gate * sig
    hidden = (active * up).astype(jnp.bfloat16)
    d_gate = (back * up * sig * (1.0 + gate * (1.0 - sig))).astype(jnp.bfloat16)
    d_up = (back * active).astype(jnp.bfloat16)
    return (hidden, d_gate, d_up)


def body(
    tokens, grad_out, gate_weight, up_weight, down_weight, gate_buffer, up_buffer, down_buffer
):
    w_gate = gate_weight[0]
    w_up = up_weight[0]
    w_down = down_weight[0]
    inputs, cotangent = (
        lax.all_gather(tokens, "col", axis=0, tiled=True),
        lax.all_gather(grad_out, "col", axis=0, tiled=True),
    )
    group_tokens = inputs.shape[0]
    gate_part = jnp.dot(inputs, w_gate, preferred_element_type=jnp.float32)
    up_part = jnp.dot(inputs, w_up, preferred_element_type=jnp.float32)
    back_part = contract_cols(cotangent, w_down)
    gate, up, back = (
        lax.psum_scatter(gate_part, "row", scatter_dimension=0, tiled=True),
        lax.psum_scatter(up_part, "row", scatter_dimension=0, tiled=True),
        lax.psum_scatter(back_part, "row", scatter_dimension=0, tiled=True),
    )
    hidden, d_gate, d_up = swiglu_grads(gate, up, back)
    hidden_all, dgate_all, dup_all = (
        lax.all_gather(hidden, "row", axis=0, tiled=True),
        lax.all_gather(d_gate, "row", axis=0, tiled=True),
        lax.all_gather(d_up, "row", axis=0, tiled=True),
    )
    replicas = lax.axis_size("rep")
    token_grad = lax.psum_scatter(
        contract_cols(dgate_all, w_gate) + contract_cols(dup_all, w_up),
        "col",
        scatter_dimension=0,
        tiled=True,
    ).astype(jnp.bfloat16)
    grad_down = contract_rows(hidden_all, cotangent) / group_tokens
    down_w, down_b = momentum_step(w_down, down_buffer[0], grad_down)
    grad_gate = contract_rows(inputs, dgate_all) / group_tokens
    grad_up = contract_rows(inputs, dup_all) / group_tokens
    gate_w, gate_b = momentum_step(w_gate, gate_buffer[0], grad_gate)
    up_w, up_b = momentum_step(w_up, up_buffer[0], grad_up)
    gate_w, up_w, gate_b, up_b = (gate_w, up_w, gate_b, up_b)
    gate_sum, up_sum, down_sum, gate_bsum, up_bsum, down_bsum = (
        lax.psum(gate_w, "rep").astype(jnp.float32),
        lax.psum(up_w, "rep").astype(jnp.float32),
        lax.psum(down_w, "rep").astype(jnp.float32),
        lax.psum(gate_b, "rep").astype(jnp.float32),
        lax.psum(up_b, "rep").astype(jnp.float32),
        lax.psum(down_b, "rep").astype(jnp.float32),
    )
    gate_new = (gate_sum / replicas).astype(jnp.bfloat16)
    up_new = (up_sum / replicas).astype(jnp.bfloat16)
    down_new = (down_sum / replicas).astype(jnp.bfloat16)
    gate_moment = (gate_bsum / replicas).astype(jnp.bfloat16)
    up_moment = (up_bsum / replicas).astype(jnp.bfloat16)
    down_moment = (down_bsum / replicas).astype(jnp.bfloat16)
    return (token_grad, gate_new, up_new, down_new, gate_moment, up_moment, down_moment)


def solution(mesh):
    return jax.shard_map(
        body,
        mesh=mesh,
        in_specs=(
            P(("rep", "col"), "row"),
            P(("rep", "col"), "row"),
            P("rep", "row", "col"),
            P("rep", "row", "col"),
            P("rep", "col", "row"),
            P("rep", "row", "col"),
            P("rep", "row", "col"),
            P("rep", "col", "row"),
        ),
        out_specs=(
            P(("rep", "col"), "row"),
            P("row", "col"),
            P("row", "col"),
            P("col", "row"),
            P("row", "col"),
            P("row", "col"),
            P("col", "row"),
        ),
        check_vma=False,
    )
```

profile of v0, /device:TPU:0, one launch (start us, length us, event | category | flops | bytes accessed | tf_op | source)
XLA Modules:
  0.0 727.0 jit_solution(10058734817589161744)
XLA Ops:
  7.2 0.0 all-gather.8.cloned.1.call-start
  7.2 0.7 all-gather.8.cloned.1.call-update
  7.9 0.0 all-gather.6.cloned.1.call-start
  7.9 0.7 all-gather.6.cloned.1.call-update
  8.6 0.0 reduce-scatter.7.cloned.1.call-start
  8.7 38.4 %all-gather.8.cloned.1.call-done = bf16[1024,1280]{1,0:T(8,128)(2,1)} async-done(((bf16[64,1280]{1,0:T(8,128)(2,1)}), bf16[1024,1280]{1,0:T(8,128)(2,1)}) %all-gather.8.cloned.1.call-update) | async-done | bytes 2621456 | tf_op jit(solution)/shard_map/all_gather | solution.py:41
  47.1 6.6 fusion.14
  53.8 0.0 copy-start.5
  53.8 0.0 reduce-scatter.7.cloned.1.call-update
  53.8 0.0 reduce-scatter.9.cloned.1.call-start
  53.8 1.7 copy-done.5
  55.5 5.9 fusion.11
  61.4 0.0 reduce-scatter.9.cloned.1.call-update
  61.4 0.0 reduce-scatter.5.cloned.1.call-start
  61.5 22.3 %all-gather.6.cloned.1.call-done = bf16[1024,1280]{1,0:T(8,128)(2,1)} async-done(((bf16[64,1280]{1,0:T(8,128)(2,1)}), bf16[1024,1280]{1,0:T(8,128)(2,1)}) %all-gather.6.cloned.1.call-update) | async-done | bytes 2621456 | tf_op jit(solution)/shard_map/all_gather | solution.py:42
  83.8 6.8 fusion.16
  90.6 0.0 reduce-scatter.5.cloned.1.call-update
  90.6 0.0 all-gather.10.cloned.1.call-start
  90.7 37.1 %reduce-scatter.7.cloned.1.call-done = f32[256,864]{0,1:T(8,128)} async-done(((f32[1024,864]{0,1:T(8,128)}), f32[256,864]{0,1:T(8,128)}) %reduce-scatter.7.cloned.1.call-update) | async-done | bytes 884752 | tf_op jit(solution)/shard_map/reduce_scatter | solution.py:50
  127.8 43.5 %reduce-scatter.9.cloned.1.call-done = f32[256,864]{0,1:T(8,128)} async-done(((f32[1024,864]{0,1:T(8,128)}), f32[256,864]{0,1:T(8,128)}) %reduce-scatter.9.cloned.1.call-update) | async-done | bytes 884752 | tf_op jit(solution)/shard_map/reduce_scatter | solution.py:49
  171.2 43.5 %reduce-scatter.5.cloned.1.call-done = f32[256,864]{0,1:T(8,128)} async-done(((f32[1024,864]{0,1:T(8,128)}), f32[256,864]{0,1:T(8,128)}) %reduce-scatter.5.cloned.1.call-update) | async-done | bytes 884752 | tf_op jit(solution)/shard_map/reduce_scatter | solution.py:51
  214.7 3.3 multiply_convert_fusion.6
  218.0 0.0 all-gather.10.cloned.1.call-update
  218.0 0.0 all-gather.12.cloned.1.call-start
  218.1 0.7 all-gather.12.cloned.1.call-update
  218.8 0.0 all-gather.14.cloned.1.call-start
  218.8 0.7 all-gather.14.cloned.1.call-update
  219.5 0.0 reduce-scatter.11.cloned.1.call-start
  219.6 30.1 %all-gather.10.cloned.1.call-done = bf16[1024,864]{0,1:T(8,128)(2,1)} async-done(((bf16[256,864]{0,1:T(8,128)(2,1)}), bf16[1024,864]{0,1:T(8,128)(2,1)}) %all-gather.10.cloned.1.call-update) | async-done | bytes 1769488 | tf_op jit(solution)/shard_map/all_gather | solution.py:56
  249.7 7.4 %fusion.9 = f32[1024,1280]{1,0:T(8,128)} fusion(bf16[1024,864]{0,1:T(8,128)(2,1)} %all-gather.10.cloned.1.call-done, bf16[1,1280,864]{1,2,0:T(8,128)(2,1)} %param.10), kind=kOutput, calls=%fused_computation.22 | convolution fusion | flops 2264924160 | bytes 9224192 | tf_op jit(solution)/shard_map/dot_general | solution.py:20
  257.1 27.6 %all-gather.12.cloned.1.call-done = bf16[1024,864]{0,1:T(8,128)(2,1)} async-done(((bf16[256,864]{0,1:T(8,128)(2,1)}), bf16[1024,864]{0,1:T(8,128)(2,1)}) %all-gather.12.cloned.1.call-update) | async-done | bytes 1769488 | tf_op jit(solution)/shard_map/all_gather | solution.py:57
  284.7 9.0 %convolution_add_fusion = f32[1024,1280]{1,0:T(8,128)} fusion(f32[1024,1280]{1,0:T(8,128)} %fusion.9, bf16[1024,864]{0,1:T(8,128)(2,1)} %all-gather.12.cloned.1.call-done, bf16[1,1280,864]{1,2,0:T(8,128)(2,1)} %param.11), kind=kOutput, calls=%fused_computation.18 | convolution fusion | flops 2266234880 | bytes 14467072 | tf_op jit(solution)/shard_map/dot_general | solution.py:20
  293.7 0.0 reduce-scatter.11.cloned.1.call-update
  293.7 0.2 all-reduce.3.cloned.1.call-start
  293.9 0.0 copy-start.6
  293.9 0.0 copy-start.7
  293.9 0.0 copy-start.8
  294.0 0.0 copy-start.9
  294.0 8.3 %fusion.6 = (bf16[1280,864]{0,1:T(8,128)(2,1)}, bf16[1280,864]{0,1:T(8,128)(2,1)}) fusion(bf16[1,1280,864]{1,2,0:T(8,128)(2,1)} %param.13, bf16[1,1280,864]{1,2,0:T(8,128)(2,1)} %param.10, bf16[1024,864]{0,1:T(8,128)(2,1)} %all-gather.10.cloned.1.call-done, bf16[1024,1280]{1,0:T(8,128)(2,1)S(1)} %copy-done.5), kind=kOutput, calls=%fused_computation.19 | convolution fusion | flops 2278195200 | bytes 13238272 | tf_op jit(solution)/shard_map/dot_general | solution.py:14
  302.3 0.0 copy-done.6
  302.3 0.0 copy-done.7
  302.3 0.0 copy-done.8
  302.3 0.0 copy-done.9
  302.3 0.0 copy-start.4
  302.3 5.3 fusion.7
  307.6 12.1 %all-gather.14.cloned.1.call-done = bf16[1024,864]{0,1:T(8,128)(2,1)} async-done(((bf16[256,864]{0,1:T(8,128)(2,1)}), bf16[1024,864]{0,1:T(8,128)(2,1)}) %all-gather.14.cloned.1.call-update) | async-done | bytes 1769488 | tf_op jit(solution)/shard_map/all_gather | solution.py:55
  319.7 0.0 copy-done.4
  319.7 8.1 %fusion.8 = (bf16[864,1280]{1,0:T(8,128)(2,1)}, bf16[864,1280]{1,0:T(8,128)(2,1)}) fusion(bf16[1,864,1280]{2,1,0:T(8,128)(2,1)} %param.15, bf16[1,864,1280]{2,1,0:T(8,128)(2,1)} %param.12, bf16[1024,864]{0,1:T(8,128)(2,1)} %all-gather.14.cloned.1.call-done, bf16[1024,1280]{1,0:T(8,128)(2,1)S(1)} %copy-done.4), kind=kOutput, calls=%fused_computation.21 | convolution fusion | flops 2278195200 | bytes 13238272 | tf_op jit(solution)/shard_map/dot_general | solution.py:14
  327.8 0.0 all-reduce.3.cloned.1.call-update
  327.9 64.1 %reduce-scatter.11.cloned.1.call-done = f32[64,1280]{1,0:T(8,128)} async-done(((f32[1024,1280]{1,0:T(8,128)}), f32[64,1280]{1,0:T(8,128)}) %reduce-scatter.11.cloned.1.call-update) | async-done | bytes 327696 | tf_op jit(solution)/shard_map/reduce_scatter | solution.py:60
  392.0 1.7 convert_element_type.89
  393.6 314.9 %all-reduce.3.cloned.1.call-done = (bf16[1280,864]{0,1:T(8,128)(2,1)}, bf16[1280,864]{0,1:T(8,128)(2,1)}, bf16[864,1280]{1,0:T(8,128)(2,1)}, bf16[1280,864]{0,1:...) async-done(((bf16[1280,864]{0,1:T(8,128)(2,1)}, bf16[1280,864]{0,1:T(8,128)(2,1)}, bf16[864,1280]{1,0:T(8,128)(2,1)}, bf16[1280,864]{0,1:T(8,128)(2,1)}, ...) | async-done | bytes 13271056 | tf_op jit(solution)/shard_map/psum | solution.py:74
  708.5 0.0 copy-start.2
  708.5 0.0 copy-start.3
  708.5 5.3 multiply_convert_fusion.4
  713.8 0.0 copy-done.2
  713.8 0.0 copy-done.3
  713.9 0.0 copy-start
  713.9 0.0 copy-start.1
  713.9 3.0 multiply_convert_fusion
  716.8 0.0 copy-done
  716.8 0.3 copy-done.1
  717.2 3.0 multiply_convert_fusion.1
Async XLA Ops:
  7.2 40.0 %all-gather.8.cloned.1.call-start = ((), (), s32[]{:S(2)}) async-start(), calls=%async_computation.6 | async-start | bytes 2785280 | tf_op jit(solution)/shard_map/all_gather | solution.py:41
  7.9 75.9 %all-gather.6.cloned.1.call-start = ((), (), s32[]{:S(2)}) async-start(), calls=%async_computation.4 | async-start | bytes 2785280 | tf_op jit(solution)/shard_map/all_gather | solution.py:42
  8.6 119.1 %reduce-scatter.7.cloned.1.call-start = ((), (), s32[]{:S(2)}) async-start(), calls=%async_computation.7 | async-start | bytes 4423680 | tf_op jit(solution)/shard_map/reduce_scatter | solution.py:50
  53.8 1.7 copy-start.5
  53.8 117.4 %reduce-scatter.9.cloned.1.call-start = ((), (), s32[]{:S(2)}) async-start(), calls=%async_computation.8 | async-start | bytes 4423680 | tf_op jit(solution)/shard_map/reduce_scatter | solution.py:49
  61.4 153.3 %reduce-scatter.5.cloned.1.call-start = ((), (), s32[]{:S(2)}) async-start(), calls=%async_computation.5 | async-start | bytes 4423680 | tf_op jit(solution)/shard_map/reduce_scatter | solution.py:51
  90.6 159.1 %all-gather.10.cloned.1.call-start = ((), (), s32[]{:S(2)}) async-start(), calls=%async_computation.9 | async-start | bytes 2211840 | tf_op jit(solution)/shard_map/all_gather | solution.py:56
  218.0 66.7 %all-gather.12.cloned.1.call-start = ((), (), s32[]{:S(2)}) async-start(), calls=%async_computation.10 | async-start | bytes 2211840 | tf_op jit(solution)/shard_map/all_gather | solution.py:57
  218.8 100.9 %all-gather.14.cloned.1.call-start = ((), (), s32[]{:S(2)}) async-start(), calls=%async_computation.12 | async-start | bytes 2211840 | tf_op jit(solution)/shard_map/all_gather | solution.py:55
  219.5 172.5 %reduce-scatter.11.cloned.1.call-start = ((), (), s32[]{:S(2)}) async-start(), calls=%async_computation.11 | async-start | bytes 5570560 | tf_op jit(solution)/shard_map/reduce_scatter | solution.py:60
  293.7 414.8 %all-reduce.3.cloned.1.call-start = ((), (), s32[]{:S(2)}) async-start(), calls=%async_computation.13 | async-start | bytes 26542080 | tf_op jit(solution)/shard_map/psum | solution.py:74
  293.9 8.4 %copy-start.6 = (bf16[1024,1280]{1,0:T(8,128)(2,1)S(1)}, bf16[1024,1280]{1,0:T(8,128)(2,1)}, u32[]{:S(2)}) copy-start(bf16[1024,1280]{1,0:T(8,128)(2,1)} %all-gather.8.cloned.1.call-done) | copy-start | bytes 7864324
  293.9 8.4 %copy-start.7 = (bf16[1,1280,864]{1,2,0:T(8,128)(2,1)S(1)}, bf16[1,1280,864]{1,2,0:T(8,128)(2,1)}, u32[]{:S(2)}) copy-start(bf16[1,1280,864]{1,2,0:T(8,128)(2,1)} %param.11) | copy-start | bytes 6635524
  293.9 8.4 %copy-start.8 = (bf16[1,1280,864]{1,2,0:T(8,128)(2,1)S(1)}, bf16[1,1280,864]{1,2,0:T(8,128)(2,1)}, u32[]{:S(2)}) copy-start(bf16[1,1280,864]{1,2,0:T(8,128)(2,1)} %param.14) | copy-start | bytes 6635524
  294.0 8.4 %copy-start.9 = (bf16[1024,864]{0,1:T(8,128)(2,1)S(1)}, bf16[1024,864]{0,1:T(8,128)(2,1)}, u32[]{:S(2)}) copy-start(bf16[1024,864]{0,1:T(8,128)(2,1)} %all-gather.12.cloned.1.call-done) | copy-start | bytes 5308420
  302.3 17.4 %copy-start.4 = (bf16[1024,1280]{1,0:T(8,128)(2,1)S(1)}, bf16[1024,1280]{1,0:T(8,128)(2,1)}, u32[]{:S(2)}) copy-start(bf16[1024,1280]{1,0:T(8,128)(2,1)} %all-gather.6.cloned.1.call-done) | copy-start | bytes 7864324
  708.5 5.3 copy-start.2
  708.5 5.3 copy-start.3
  713.9 3.0 copy-start
  713.9 3.3 copy-start.1
Sparse Core Ops, SparseCore 0:
  9.7 37.3 all-gather.7
  48.8 34.9 all-gather.5
  86.3 41.4 reduce-scatter.6
  130.0 41.1 reduce-scatter.8
  173.5 41.1 reduce-scatter.4
  218.2 31.4 all-gather.9
  251.9 32.7 all-gather.11
  286.9 32.7 all-gather.13
  322.1 69.8 reduce-scatter.10
  395.7 312.7 all-reduce.2
where the time goes:
time: 728 us; the launch traced here: 727 us
  waiting for transfers between devices  636 us (87%)
  matrix products  57.5 us (8%)
  other arithmetic  16.2 us (2%)
  between operations  14.2 us (2%)
    psum x1, waiting for transfers between devices, body(): lax.psum(gate_w, 'rep').astype(jnp.float32)  315 us
    reduce_scatter x1, waiting for transfers between devices, body(): lax.psum_scatter(contract_cols(dgate_all, w_gate) + contract_cols(dup_all...  64.1 us
    reduce_scatter x1, waiting for transfers between devices, body(): lax.psum_scatter(gate_part, 'row', scatter_dimension=0, tiled=True)  43.5 us
    reduce_scatter x1, waiting for transfers between devices, body(): lax.psum_scatter(back_part, 'row', scatter_dimension=0, tiled=True)  43.5 us
    all_gather x1, waiting for transfers between devices, body(): lax.all_gather(tokens, 'col', axis=0, tiled=True)  38.4 us
    reduce_scatter x1, waiting for transfers between devices, body(): lax.psum_scatter(up_part, 'row', scatter_dimension=0, tiled=True)  37.1 us
    all_gather x1, waiting for transfers between devices, body(): lax.all_gather(d_gate, 'row', axis=0, tiled=True)  30.1 us
    all_gather x1, waiting for transfers between devices, body(): lax.all_gather(d_up, 'row', axis=0, tiled=True)  27.6 us
  transfers between devices with their start and end apart: 10, of which 10 were waited for; matrix products, arithmetic and copies ran while one was open for 8% of the time, Pallas kernels for 0%

commit v1 on v0

v1 whole, which is shorter than its diff:
```python
import functools

import jax
import jax.numpy as jnp
from jax import lax
from jax.experimental import pallas as pl
from jax.experimental.pallas import tpu as pltpu
from jax.sharding import PartitionSpec as P

MESH = pl.DeviceIdType.MESH
F32, BF16 = jnp.float32, jnp.bfloat16

TOK = 1024
D = 1280
F = 864
BLK = 64
CH = 256
NP = D // CH
STEP = 16
STEP_D = 48
MIX = 1.85
LEAD = 1.35


def rows_of(i, n):
    return pl.ds(pl.multiple_of(i * n, n), n)


def contract(a, b, dim_a, dim_b):
    return lax.dot_general(
        a, b, (((dim_a,), (dim_b,)), ((), ())), preferred_element_type=F32
    )


def rebuild(lam):
    keep = 1.0 - lam
    return keep, lam - MIX * keep, lam / MIX, keep - lam / MIX


def kernel(
    x_in, g_in, wg_in, wu_in, wd_in, bg_in, bu_in, bd_in,
    tg_out, gw_out, uw_out, dw_out, gb_out, ub_out, db_out, qr_gu, qr_d, pr_gu, pr_d,
    xs, gs, wg, wu, wd, q_gu, q_d, stg, own_b, rcv, hid, dgt, dup,
    tp, tc, ty, tzs, tz, tgo, gt, gt_d, cin, cin_d, out, out_d, lam_l, lam_r,
    ld_s, b_s, tok_s, tok_r, q_s, q_r, p_s, p_r, lam_s, rs_s, rs_r, ag_s, ag_r,
    tc_s, ty_s, ty_r, tz_s, cin_s, out_s, tg_s,
):
    r, x, c = lax.axis_index("rep"), lax.axis_index("row"), lax.axis_index("col")
    k = lax.rem(c, 2)
    y = lax.rem(c // 2, 4)
    zl = c // 8

    def col_of(zl_, y_, k_):
        return zl_ * 8 + y_ * 2 + k_

    peer = (1 - r, x, c)
    sib = (r, x, col_of(zl, y, 1 - k))
    zn = (r, x, col_of(1 - zl, y, k))
    ydev = {d: (r, x, col_of(zl, lax.rem(y + d, 4), k)) for d in (1, 2, 3)}

    def xdev(d):
        return (r, lax.rem(x + d, 4), c)

    def load(src, dst, i):
        return pltpu.make_async_copy(src, dst, ld_s.at[i])

    own_rows = rows_of(c, BLK)
    loads = [
        load(x_in, xs.at[own_rows], 0),
        load(g_in, gs.at[own_rows], 1),
        load(wd_in, wd, 2),
        load(wg_in, wg, 3),
        load(wu_in, wu, 4),
    ]
    for cp in loads:
        cp.start()

    def load_b(src, p, s):
        return pltpu.make_async_copy(src.at[rows_of(p, CH)], cin.at[s], b_s.at[s])

    def load_bd(p, s):
        return pltpu.make_async_copy(bd_in.at[:, rows_of(p, CH)], cin_d.at[s], b_s.at[s])

    for s in range(2):
        load_bd(s, s).start()

    bar = pltpu.get_barrier_semaphore()
    partners = [peer, sib, zn] + [ydev[d] for d in (1, 2, 3)] + [xdev(d) for d in (1, 2, 3)]
    for dev in partners:
        pl.semaphore_signal(bar, 1, device_id=dev, device_id_type=MESH)
    pl.semaphore_wait(bar, len(partners))

    def remote(src, dst, ss, rs, dev):
        return pltpu.make_async_remote_copy(
            src_ref=src, dst_ref=dst, send_sem=ss, recv_sem=rs, device_id=dev, device_id_type=MESH
        )

    mats = (xs, gs)

    def tok(m, owner, n, dev):
        blk = mats[m].at[rows_of(owner, BLK)]
        return remote(blk, blk, tok_s.at[m, n], tok_r.at[m, owner], dev)

    zn_owner = col_of(1 - zl, y, k)
    y_owner = {d: col_of(zl, lax.rem(y + 4 - d, 4), k) for d in (1, 2, 3)}
    zy_owner = {d: col_of(1 - zl, lax.rem(y + 4 - d, 4), k) for d in (1, 2, 3)}

    def tok_list(m):
        return (
            [(c, 1, zn), (c, 0, sib)]
            + [(c, 1 + d, ydev[d]) for d in (1, 2, 3)]
            + [(zn_owner, 5 + d, ydev[d]) for d in (1, 2, 3)]
            + [(zn_owner, 5, sib)]
            + [(y_owner[d], 8 + d, sib) for d in (1, 2, 3)]
            + [(zy_owner[d], 11 + d, sib) for d in (1, 2, 3)]
        )

    sends = [tok_list(0), tok_list(1)]

    def tok_start(m, lo, hi):
        for owner, n, dev in sends[m][lo:hi]:
            tok(m, owner, n, dev).start()

    def tok_wait(m, owner):
        tok(m, owner, 0, sib).wait_recv()

    for m in range(2):
        loads[m].wait()
        tok_start(m, 0, 5)

    def squares(w, b):
        u = w - 0.315 * b
        v = (0.9 * MIX) * b
        return u * u, v * v

    def fold(v, lanes):
        return jnp.sum(v.reshape(v.shape[0] // 8, 8, lanes), axis=0)

    def choose(t, su, sv):
        lam = (jnp.sum(sv, keepdims=True) > jnp.sum(su, keepdims=True)).astype(F32)
        lam_l[t] = jnp.broadcast_to(lam, (8, 128))

    def q_copy_d(p):
        return remote(q_d.at[p], qr_d.at[p], q_s.at[p], q_r.at[p], peer)

    def q_copy(t, p):
        i = t * NP + p
        return remote(q_gu.at[i - NP], qr_gu.at[i - NP], q_s.at[i], q_r.at[i], peer)

    loads[2].wait()

    def q_down(p, carry):
        s = lax.rem(p, 2)
        load_bd(p, s).wait()

        def inner(i, acc):
            rr = rows_of(i, STEP_D)
            w = wd[rr, rows_of(p, CH)].astype(F32)
            b = cin_d[s, rr].astype(F32)
            q_d[p, rr] = (w + LEAD * b).astype(BF16)
            uu, vv = squares(w, b)
            return acc[0] + fold(uu, CH), acc[1] + fold(vv, CH)

        carry = lax.fori_loop(0, F // STEP_D, inner, carry)
        q_copy_d(p).start()

        @pl.when(p + 2 < NP)
        def _():
            load_bd(p + 2, s).start()

        return carry

    zero_d = jnp.zeros((8, CH), F32)
    choose(0, *lax.fori_loop(0, NP, q_down, (zero_d, zero_d)))

    def q_matrix(t, w_ref, b_in):
        for s in range(2):
            load_b(b_in, s, s).start()
        loads[2 + t].wait()

        def piece(p, carry):
            s = lax.rem(p, 2)
            load_b(b_in, p, s).wait()

            def inner(i, acc):
                rr = rows_of(i, STEP)
                w = w_ref[pl.ds(pl.multiple_of(p * CH + i * STEP, STEP), STEP)].astype(F32)
                b = cin[s, rr].astype(F32)
                q_gu[p + (t - 1) * NP, rr] = (w + LEAD * b).astype(BF16)
                uu, vv = squares(w, b)
                return acc[0] + fold(uu, F), acc[1] + fold(vv, F)

            carry = lax.fori_loop(0, CH // STEP, inner, carry)
            q_copy(t, p).start()

            @pl.when(p + 2 < NP)
            def _():
                load_b(b_in, p + 2, s).start()

            return carry

        zero = jnp.zeros((8, F), F32)
        choose(t, *lax.fori_loop(0, NP, piece, (zero, zero)))

    q_matrix(1, wg, bg_in)
    q_matrix(2, wu, bu_in)
    lam_copy = remote(lam_l, lam_r, lam_s.at[0], lam_s.at[1], peer)
    lam_copy.start()

    def forward_near(m):
        tok_wait(m, zn_owner)
        tok_start(m, 5, 9)
        for i, d in enumerate((1, 2, 3)):
            tok_wait(m, y_owner[d])
            tok_start(m, 9 + i, 10 + i)

    def forward_far(m):
        for i, d in enumerate((1, 2, 3)):
            tok_wait(m, zy_owner[d])
            tok_start(m, 12 + i, 13 + i)

    def from_sibling(m):
        for i in range(8):
            tok_wait(m, 2 * i + 1 - k)

    forward_near(0)
    forward_near(1)
    forward_far(0)
    from_sibling(0)

    def rs_copy(t, src, d):
        return remote(src, rcv.at[t, d - 1], rs_s.at[t, d - 1], rs_r.at[t, d - 1], xdev(d))

    def partial_in(t, w_ref):
        def step(i, _):
            j = lax.rem(x + i + 1, 4)
            stg[t, i] = jnp.dot(xs[rows_of(j, CH)], w_ref[...], preferred_element_type=F32)

            @pl.when(i < 3)
            def _():
                rs_copy(t, stg.at[t, i], i + 1).start()

            return 0

        lax.fori_loop(0, 4, step, 0)

    partial_in(0, wg)
    partial_in(1, wu)
    forward_far(1)
    from_sibling(1)

    for t in range(2):
        for d in (1, 2, 3):
            rs_copy(t, stg.at[t, d - 1], d).wait()

    def ag_copy(t, d, start=True):
        ref = (hid, dgt, dup)[t]
        rr = rows_of(x, CH)
        return remote(ref.at[rr], ref.at[rr], ag_s.at[t, d - 1], ag_r.at[t, d - 1], xdev(d))

    def ag_wait(t):
        ref = (hid, dgt, dup)[t]
        for d in (1, 2, 3):
            rr = rows_of(lax.rem(x + 4 - d, 4), CH)
            remote(ref.at[rr], ref.at[rr], ag_s.at[t, d - 1], ag_r.at[t, d - 1], xdev(d)).wait_recv()

    def make_hidden(i, _):
        rr = rows_of(i, STEP)
        gate = ((stg[0, 3, rr] + rcv[0, 0, rr]) + rcv[0, 1, rr]) + rcv[0, 2, rr]
        up = ((stg[1, 3, rr] + rcv[1, 0, rr]) + rcv[1, 1, rr]) + rcv[1, 2, rr]
        sig = jax.nn.sigmoid(gate)
        stg[0, 3, rr] = gate
        stg[1, 3, rr] = up
        hid[pl.ds(pl.multiple_of(x * CH + i * STEP, STEP), STEP)] = (gate * sig * up).astype(BF16)
        return 0

    lax.fori_loop(0, CH // STEP, make_hidden, 0)
    for d in (1, 2, 3):
        ag_copy(0, d).start()

    def partial_back(i, _):
        j = lax.rem(x + i + 1, 4)
        stg[0, i] = contract(gs[rows_of(j, CH)], wd[...], 1, 1)
        rs_copy(2, stg.at[0, i], i + 1).start()
        return 0

    lax.fori_loop(0, 3, partial_back, 0)
    own_b[...] = contract(gs[rows_of(x, CH)], wd[...], 1, 1)

    def p_copy_d(p):
        return remote(wd.at[:, rows_of(p, CH)], pr_d.at[p], p_s.at[p], p_r.at[p], peer)

    def p_copy(t, p):
        w_ref = (wg, wu)[t - 1]
        i = t * NP + p
        return remote(w_ref.at[rows_of(p, CH)], pr_gu.at[i - NP], p_s.at[i], p_r.at[i], peer)

    def moment(w, b, g, lam):
        g = g * (1.0 / TOK)
        new_b = 0.9 * b + 0.1 * g
        new_w = w - 0.5 * (0.3 * g + 0.7 * new_b)
        return jnp.where(lam > 0.5, new_w, new_b).astype(BF16)

    def step_down():
        for s in range(2):
            load_bd(s, s).start()
        lam = lam_l[0, 0:1, 0:1]

        def piece(p, _):
            cols = rows_of(p, CH)
            s = lax.rem(p, 2)
            gt_d[...] = contract(hid[...], gs[:, cols], 0, 0)
            load_bd(p, s).wait()

            def inner(i, _):
                rr = rows_of(i, STEP_D)
                w, b = wd[rr, cols].astype(F32), cin_d[s, rr].astype(F32)
                wd[rr, cols] = moment(w, b, gt_d[rr], lam)
                return 0

            lax.fori_loop(0, F // STEP_D, inner, 0)
            p_copy_d(p).start()

            @pl.when(p + 2 < NP)
            def _():
                load_bd(p + 2, s).start()

            return 0

        lax.fori_loop(0, NP, piece, 0)

    def step_matrix(t, w_ref, b_in, grads):
        for s in range(2):
            load_b(b_in, s, s).start()
        lam = lam_l[t, 0:1, 0:1]

        def piece(p, _):
            s = lax.rem(p, 2)
            gt[...] = contract(xs[:, rows_of(p, CH)], grads[...], 0, 0)
            load_b(b_in, p, s).wait()

            def inner(i, _):
                rr = rows_of(i, STEP)
                wr = pl.ds(pl.multiple_of(p * CH + i * STEP, STEP), STEP)
                w, b = w_ref[wr].astype(F32), cin[s, rr].astype(F32)
                w_ref[wr] = moment(w, b, gt[rr], lam)
                return 0

            lax.fori_loop(0, CH // STEP, inner, 0)
            p_copy(t, p).start()

            @pl.when(p + 2 < NP)
            def _():
                load_b(b_in, p + 2, s).start()

            return 0

        lax.fori_loop(0, NP, piece, 0)

    ag_wait(0)
    step_down()

    for d in (1, 2, 3):
        rs_copy(2, stg.at[0, d - 1], d).wait()

    def make_grads(i, _):
        rr = rows_of(i, STEP)
        back = ((own_b[rr] + rcv[2, 0, rr]) + rcv[2, 1, rr]) + rcv[2, 2, rr]
        gate, up = stg[0, 3, rr], stg[1, 3, rr]
        sig = jax.nn.sigmoid(gate)
        wr = pl.ds(pl.multiple_of(x * CH + i * STEP, STEP), STEP)
        dgt[wr] = (back * up * sig * (1.0 + gate * (1.0 - sig))).astype(BF16)
        dup[wr] = (back * (gate * sig)).astype(BF16)
        return 0

    lax.fori_loop(0, CH // STEP, make_grads, 0)
    for t in (1, 2):
        for d in (1, 2, 3):
            ag_copy(t, d).start()

    def token_part(grads, w_ref, first):
        def step(j, _):
            part = contract(grads[rows_of(j, CH)], w_ref[...], 1, 1).reshape(2, 2, BLK, D)
            two = rows_of(j, 2)
            if first:
                tp[two] = part
            else:
                tp[two] = tp[two] + part
            return 0

        lax.fori_loop(0, 4, step, 0)

    ag_wait(1)
    token_part(dgt, wg, True)
    step_matrix(1, wg, bg_in, dgt)
    ag_wait(2)
    token_part(dup, wu, False)
    tc_copy = remote(tp.at[:, 1 - k], tc, tc_s.at[0], tc_s.at[1], sib)
    tc_copy.start()
    step_matrix(2, wu, bu_in, dup)

    lam_copy.wait()

    def means(t, q_a, p_a, q_b, p_b):
        la = rebuild(lam_l[t, 0:1, 0:1])
        lb = rebuild(lam_r[t, 0:1, 0:1])
        q_a, p_a, q_b, p_b = (v.astype(F32) for v in (q_a, p_a, q_b, p_b))
        w = (la[0] * q_a + la[1] * p_a) + (lb[0] * q_b + lb[1] * p_b)
        b = (la[2] * q_a + la[3] * p_a) + (lb[2] * q_b + lb[3] * p_b)
        return (0.5 * w).astype(BF16), (0.5 * b).astype(BF16)

    def out_copy_d(p, s):
        cols = rows_of(p, CH)
        return (
            pltpu.make_async_copy(out_d.at[s, 0], dw_out.at[:, cols], out_s.at[s, 0]),
            pltpu.make_async_copy(out_d.at[s, 1], db_out.at[:, cols], out_s.at[s, 1]),
        )

    def combine_down():
        def piece(p, _):
            s = lax.rem(p, 2)
            q_copy_d(p).wait()
            p_copy_d(p).wait()
            ins = (
                pltpu.make_async_copy(qr_d.at[p], cin_d.at[0], cin_s.at[0]),
                pltpu.make_async_copy(pr_d.at[p], cin_d.at[1], cin_s.at[1]),
            )
            for cp in ins:
                cp.start()

            @pl.when(p >= 2)
            def _():
                for cp in out_copy_d(p - 2, s):
                    cp.wait()

            for cp in ins:
                cp.wait()

            def inner(i, _):
                rr = rows_of(i, STEP_D)
                w, b = means(0, q_d[p, rr], wd[rr, rows_of(p, CH)], cin_d[0, rr], cin_d[1, rr])
                out_d[s, 0, rr] = w
                out_d[s, 1, rr] = b
                return 0

            lax.fori_loop(0, F // STEP_D, inner, 0)
            for cp in out_copy_d(p, s):
                cp.start()
            return 0

        lax.fori_loop(0, NP, piece, 0)
        for p in (NP - 2, NP - 1):
            for cp in out_copy_d(p, p % 2):
                cp.wait()

    def combine(t, w_ref, w_out, b_out):
        def out_copy(p, s):
            rr = rows_of(p, CH)
            return (
                pltpu.make_async_copy(out.at[s, 0], w_out.at[rr], out_s.at[s, 0]),
                pltpu.make_async_copy(out.at[s, 1], b_out.at[rr], out_s.at[s, 1]),
            )

        def piece(p, _):
            s = lax.rem(p, 2)
            i = p + (t - 1) * NP
            q_copy(t, p).wait()
            p_copy(t, p).wait()
            ins = (
                pltpu.make_async_copy(qr_gu.at[i], cin.at[0], cin_s.at[0]),
                pltpu.make_async_copy(pr_gu.at[i], cin.at[1], cin_s.at[1]),
            )
            for cp in ins:
                cp.start()

            @pl.when(p >= 2)
            def _():
                for cp in out_copy(p - 2, s):
                    cp.wait()

            for cp in ins:
                cp.wait()

            def inner(n, _):
                rr = rows_of(n, STEP)
                wr = pl.ds(pl.multiple_of(p * CH + n * STEP, STEP), STEP)
                w, b = means(t, q_gu[i, rr], w_ref[wr], cin[0, rr], cin[1, rr])
                out[s, 0, rr] = w
                out[s, 1, rr] = b
                return 0

            lax.fori_loop(0, CH // STEP, inner, 0)
            for cp in out_copy(p, s):
                cp.start()
            return 0

        lax.fori_loop(0, NP, piece, 0)
        for p in (NP - 2, NP - 1):
            for cp in out_copy(p, p % 2):
                cp.wait()

    tc_copy.wait()

    def add_core(i, _):
        tc[i] = tc[i] + tp[i, k]
        return 0

    lax.fori_loop(0, 8, add_core, 0)

    def ty_copy(d, half):
        to = half * 4 + lax.rem(y + d, 4)
        return remote(tc.at[to], ty.at[d - 1, half], ty_s.at[d - 1, half], ty_r.at[d - 1, half], ydev[d])

    for d in (1, 2, 3):
        for half in range(2):
            ty_copy(d, half).start()

    combine_down()

    for d in (1, 2, 3):
        for half in range(2):
            ty_copy(d, half).wait()

    def along_y(half):
        return ((tc[half * 4 + y] + ty[0, half]) + ty[1, half]) + ty[2, half]

    tzs[...] = along_y(1 - zl).astype(BF16)
    tz_copy = remote(tzs, tz, tz_s.at[0], tz_s.at[1], zn)
    tz_copy.start()

    combine(1, wg, gw_out, gb_out)

    tz_copy.wait()
    tgo[...] = (along_y(zl) + tz[...].astype(F32)).astype(BF16)
    tg_copy = pltpu.make_async_copy(tgo, tg_out, tg_s.at[0])
    tg_copy.start()

    combine(2, wu, uw_out, ub_out)

    tg_copy.wait()
    for m in range(2):
        for owner, n, dev in sends[m]:
            tok(m, owner, n, dev).wait_send()
    for t in range(3):
        for d in (1, 2, 3):
            ag_copy(t, d).wait_send()


def body(tokens, grad_out, wg, wu, wd, bg, bu, bd):
    dma = pltpu.SemaphoreType.DMA
    whole = [(BLK, D)] + [(D, F), (D, F), (F, D)] * 2
    slots = [(2 * NP, CH, F), (NP, F, CH)] * 2
    scratch = [
        pltpu.VMEM((TOK, D), BF16),
        pltpu.VMEM((TOK, D), BF16),
        pltpu.VMEM((D, F), BF16),
        pltpu.VMEM((D, F), BF16),
        pltpu.VMEM((F, D), BF16),
        pltpu.VMEM((2 * NP, CH, F), BF16),
        pltpu.VMEM((NP, F, CH), BF16),
        pltpu.VMEM((2, 4, CH, F), F32),
        pltpu.VMEM((CH, F), F32),
        pltpu.VMEM((3, 3, CH, F), F32),
        pltpu.VMEM((TOK, F), BF16),
        pltpu.VMEM((TOK, F), BF16),
        pltpu.VMEM((TOK, F), BF16),
        pltpu.VMEM((8, 2, BLK, D), F32),
        pltpu.VMEM((8, BLK, D), F32),
        pltpu.VMEM((3, 2, BLK, D), F32),
        pltpu.VMEM((BLK, D), BF16),
        pltpu.VMEM((BLK, D), BF16),
        pltpu.VMEM((BLK, D), BF16),
        pltpu.VMEM((CH, F), F32),
        pltpu.VMEM((F, CH), F32),
        pltpu.VMEM((2, CH, F), BF16),
        pltpu.VMEM((2, F, CH), BF16),
        pltpu.VMEM((2, 2, CH, F), BF16),
        pltpu.VMEM((2, 2, F, CH), BF16),
        pltpu.VMEM((3, 8, 128), F32),
        pltpu.VMEM((3, 8, 128), F32),
        dma((5,)),
        dma((2,)),
        dma((2, 15)),
        dma((2, 16)),
        dma((3 * NP,)),
        dma((3 * NP,)),
        dma((3 * NP,)),
        dma((3 * NP,)),
        dma((2,)),
        dma((3, 3)),
        dma((3, 3)),
        dma((3, 3)),
        dma((3, 3)),
        dma((2,)),
        dma((3, 2)),
        dma((3, 2)),
        dma((2,)),
        dma((2,)),
        dma((2, 2)),
        dma((1,)),
    ]
    res = pl.pallas_call(
        kernel,
        out_shape=[jax.ShapeDtypeStruct(s, BF16) for s in whole + slots],
        in_specs=[pl.BlockSpec(memory_space=pl.ANY)] * 8,
        out_specs=[pl.BlockSpec(memory_space=pl.ANY)] * 11,
        scratch_shapes=scratch,
        compiler_params=pltpu.CompilerParams(
            collective_id=0, has_side_effects=True, vmem_limit_bytes=63 * 2**20
        ),
        cost_estimate=pl.CostEstimate(
            flops=16 * TOK * D * F, bytes_accessed=40 * D * F, transcendentals=2 * CH * F
        ),
    )(tokens, grad_out, wg[0], wu[0], wd[0], bg[0], bu[0], bd[0])
    return tuple(res[:7])


def solution(mesh):
    weights = (P("rep", "row", "col"), P("rep", "row", "col"), P("rep", "col", "row"))
    means = (P("row", "col"), P("row", "col"), P("col", "row"))
    return jax.shard_map(
        body,
        mesh=mesh,
        in_specs=(P(("rep", "col"), "row"),) * 2 + weights * 2,
        out_specs=(P(("rep", "col"), "row"),) + means * 2,
        check_vma=False,
    )
```

time: 728 us -> 360 us (0.49)
  waiting for transfers between devices: 636 us -> 0 us
  Pallas kernels: 0 us -> 324 us
  matrix products: 57.5 us -> 0 us
  local copies, waits for them, and re-layouts: 2.05 us -> 34.2 us
  other arithmetic: 16.2 us -> 0 us
  between operations: 14.2 us -> 0.67 us
    pallas_call x0 -> x1, Pallas kernels: none -> 324 us  [body(): pl.pallas_call(kernel, out_shape=[jax.ShapeDtypeStruct(s, BF16) for s in...]
    psum x1 -> x0, waiting for transfers between devices: 315 us -> none  [body(): lax.psum(gate_w, 'rep').astype(jnp.float32)]
    reduce_scatter x4 -> x0, waiting for transfers between devices: 188 us -> none  [the longest x1 64.1 us: body(): lax.psum_scatter(contract_cols(dgate_all, w_gate) + contract_cols(dup_all...]
    all_gather x5 -> x0, waiting for transfers between devices: 131 us -> none  [the longest x1 38.4 us: body(): lax.all_gather(tokens, 'col', axis=0, tiled=True)]
    dot_general x8 -> x0, matrix products: 57.5 us -> none  [the longest x3 23.2 us: contract_cols(): lax.dot_general(left, right, (((1,), (1,)), ((), ())), preferred_element_...]
    unnamed x20 -> x23, local copies, waits for them, and re-layouts: 2.05 us -> 34.2 us
    convert_element_type x5 -> x0, other arithmetic: 16.2 us -> none  [the longest x1 5.34 us: body(): up_new = (up_sum / replicas).astype(jnp.bfloat16)]
  transfers between devices with their start and end apart: 10 -> 0, of which waited for: 10 -> 0; matrix products, arithmetic and copies ran while one was open for 8% -> 0% of each run, Pallas kernels for 0% -> 0%
where the time goes in v1:
time: 360 us; the launch traced here: 358 us
  Pallas kernels  324 us (90%)
  local copies, waits for them, and re-layouts  34.2 us (10%)
    pallas_call x1, Pallas kernels, body(): pl.pallas_call(kernel, out_shape=[jax.ShapeDtypeStruct(s, BF16) for s in...  324 us
    unnamed x23, local copies, waits for them, and re-layouts  34.2 us

profile of v1, /device:TPU:0, one launch (start us, length us, event | category | flops | bytes accessed | tf_op | source)
XLA Modules:
  0.0 358.4 jit_solution(10542429781858210738)
XLA Ops:
  0.6 0.0 copy-start.2
  0.6 4.5 %copy.15 = bf16[1,1280,864]{2,1,0:T(8,128)(2,1)} copy(bf16[1,1280,864]{1,2,0:T(8,128)(2,1)} %param.10) | data formatting | bytes 4423680 | tf_op args[2]
  5.1 0.0 copy-done.2
  5.1 3.3 copy.16
  8.4 0.0 copy-start.3
  8.4 4.5 %copy.17 = bf16[1,1280,864]{2,1,0:T(8,128)(2,1)} copy(bf16[1,1280,864]{1,2,0:T(8,128)(2,1)} %param.13) | data formatting | bytes 4423680 | tf_op args[5]
  12.9 0.0 copy-done.3
  12.9 3.2 copy.18
  16.1 323.5 %shard_map.135 = (bf16[64,1280]{1,0:T(8,128)(2,1)}, bf16[1280,864]{1,0:T(8,128)(2,1)}, bf16[1280,864]{1,0:T(8,128)(2,1)}, bf16[864,1280]{1,0:T(8,128)(2,1)}, bf1...) custom-call(bf16[64,1280]{1,0:T(8,128)(2,1)} %x_in.1, ...), custom_call_target="tpu_custom_call" | custom-call | flops 18119393280 | bytes 44236800 | tf_op jit(solution)/shard_map/pallas_call | solution.py:602
  339.6 0.0 copy-start.1
  339.6 4.3 %copy.19 = bf16[1280,864]{0,1:T(8,128)(2,1)} copy(bf16[1280,864]{1,0:T(8,128)(2,1)} %get-tuple-element.22) | data formatting | bytes 4423680
  343.9 0.0 copy-done.1
  343.9 2.5 copy.20
  346.4 0.0 copy-start
  346.4 4.3 %copy.21 = bf16[1280,864]{0,1:T(8,128)(2,1)} copy(bf16[1280,864]{1,0:T(8,128)(2,1)} %get-tuple-element.25) | data formatting | bytes 4423680
  350.6 0.0 copy-done
  350.6 0.0 copy-start.5
  350.6 2.5 copy.22
  353.1 0.0 copy-done.5
  353.1 0.7 copy.26
  353.8 0.0 copy-start.4
  353.8 3.3 copy.27
  357.1 0.0 copy-done.4
  357.1 1.4 copy.28
Async XLA Ops:
  0.6 4.5 %copy-start.2 = (bf16[1,1280,864]{1,2,0:T(8,128)(2,1)S(1)}, bf16[1,1280,864]{1,2,0:T(8,128)(2,1)}, u32[]{:S(2)}) copy-start(bf16[1,1280,864]{1,2,0:T(8,128)(2,1)} %param.11) | copy-start | bytes 6635524
  8.4 4.5 %copy-start.3 = (bf16[1,1280,864]{1,2,0:T(8,128)(2,1)S(1)}, bf16[1,1280,864]{1,2,0:T(8,128)(2,1)}, u32[]{:S(2)}) copy-start(bf16[1,1280,864]{1,2,0:T(8,128)(2,1)} %param.14) | copy-start | bytes 6635524
  339.6 4.3 %copy-start.1 = (bf16[1280,864]{1,0:T(8,128)(2,1)S(1)}, bf16[1280,864]{1,0:T(8,128)(2,1)}, u32[]{:S(2)}) copy-start(bf16[1280,864]{1,0:T(8,128)(2,1)} %get-tuple-element.23) | copy-start | bytes 6635524
  346.4 4.3 %copy-start = (bf16[1280,864]{1,0:T(8,128)(2,1)S(1)}, bf16[1280,864]{1,0:T(8,128)(2,1)}, u32[]{:S(2)}) copy-start(bf16[1280,864]{1,0:T(8,128)(2,1)} %get-tuple-element.26) | copy-start | bytes 6635524
  350.6 2.5 copy-start.5
  353.8 3.3 copy-start.4

commit v2 on v1

v2 whole, which is shorter than its diff:
```python
import functools

import jax
import jax.numpy as jnp
from jax import lax
from jax.experimental import pallas as pl
from jax.experimental.pallas import tpu as pltpu
from jax.sharding import PartitionSpec as P

MESH = pl.DeviceIdType.MESH
F32, BF16 = jnp.float32, jnp.bfloat16

TOK = 1024
D = 1280
F = 864
BLK = 64
CH = 256
NP = D // CH
STEP = 16
STEP_D = 48
MIX = 1.85
LEAD = 1.35


def rows_of(i, n):
    return pl.ds(pl.multiple_of(i * n, n), n)


def contract(a, b, dim_a, dim_b):
    return lax.dot_general(
        a, b, (((dim_a,), (dim_b,)), ((), ())), preferred_element_type=F32
    )


def rebuild(lam):
    keep = 1.0 - lam
    return keep, lam - MIX * keep, lam / MIX, keep - lam / MIX


def kernel(
    x_in, g_in, wg_in, wu_in, wd_in, bg_in, bu_in, bd_in,
    tgo, wg, wu, wd, qg, qu, qd, qr,
    xs, gs, pr, stg, own_b, rcv, hid, dgt, dup,
    tp, tc, ty, tzs, tz, gt, cin, lam_l, lam_r,
    ld_s, b_s, tok_s, tok_r, q_s, q_r, p_s, p_r, lam_s, rs_s, rs_r, ag_s, ag_r,
    tc_s, ty_s, ty_r, tz_s, cin_s,
):
    r, x, c = lax.axis_index("rep"), lax.axis_index("row"), lax.axis_index("col")
    k = lax.rem(c, 2)
    y = lax.rem(c // 2, 4)
    zl = c // 8

    ws, qs = (wd, wg, wu), (qd, qg, qu)

    def col_of(zl_, y_, k_):
        return zl_ * 8 + y_ * 2 + k_

    peer = (1 - r, x, c)
    sib = (r, x, col_of(zl, y, 1 - k))
    zn = (r, x, col_of(1 - zl, y, k))
    ydev = {d: (r, x, col_of(zl, lax.rem(y + d, 4), k)) for d in (1, 2, 3)}

    def xdev(d):
        return (r, lax.rem(x + d, 4), c)

    bar = pltpu.get_barrier_semaphore()
    partners = [peer, sib, zn] + [ydev[d] for d in (1, 2, 3)] + [xdev(d) for d in (1, 2, 3)]
    for dev in partners:
        pl.semaphore_signal(bar, 1, device_id=dev, device_id_type=MESH)

    def load(src, dst, i):
        return pltpu.make_async_copy(src, dst, ld_s.at[i])

    own_rows = rows_of(c, BLK)
    loads = [
        load(x_in, xs.at[own_rows], 0),
        load(g_in, gs.at[own_rows], 1),
        load(wd_in, wd, 2),
        load(wg_in, wg, 3),
        load(wu_in, wu, 4),
    ]
    for cp in loads:
        cp.start()

    bs = (bd_in, bg_in, bu_in)

    def load_b(t, p, s):
        return pltpu.make_async_copy(bs[t].at[:, rows_of(p, CH)], cin.at[s], b_s.at[s])

    for s in range(2):
        load_b(0, s, s).start()

    def remote(src, dst, ss, rs, dev):
        return pltpu.make_async_remote_copy(
            src_ref=src, dst_ref=dst, send_sem=ss, recv_sem=rs, device_id=dev, device_id_type=MESH
        )

    mats = (xs, gs)

    def tok(m, owner, n, dev):
        blk = mats[m].at[rows_of(owner, BLK)]
        return remote(blk, blk, tok_s.at[m, n], tok_r.at[m, owner], dev)

    zn_owner = col_of(1 - zl, y, k)
    y_owner = {d: col_of(zl, lax.rem(y + 4 - d, 4), k) for d in (1, 2, 3)}
    zy_owner = {d: col_of(1 - zl, lax.rem(y + 4 - d, 4), k) for d in (1, 2, 3)}

    def tok_list(m):
        return (
            [(c, 1, zn), (c, 0, sib)]
            + [(c, 1 + d, ydev[d]) for d in (1, 2, 3)]
            + [(zn_owner, 5 + d, ydev[d]) for d in (1, 2, 3)]
            + [(zn_owner, 5, sib)]
            + [(y_owner[d], 8 + d, sib) for d in (1, 2, 3)]
            + [(zy_owner[d], 11 + d, sib) for d in (1, 2, 3)]
        )

    sends = [tok_list(0), tok_list(1)]

    def tok_start(m, lo, hi):
        for owner, n, dev in sends[m][lo:hi]:
            tok(m, owner, n, dev).start()

    def tok_wait(m, owner):
        tok(m, owner, 0, sib).wait_recv()

    def squares(w, b):
        u = w - 0.315 * b
        v = (0.9 * MIX) * b
        return u * u, v * v

    def fold(v):
        return jnp.sum(v.reshape(STEP_D // 8, 8, CH), axis=0)

    def q_copy(t, p):
        i = t * NP + p
        return remote(qs[t].at[:, rows_of(p, CH)], qr.at[i], q_s.at[i], q_r.at[i], peer)

    def q_piece(t, p, carry):
        s = lax.rem(p, 2)
        cols = rows_of(p, CH)
        load_b(t, p, s).wait()

        def inner(i, acc):
            rr = rows_of(i, STEP_D)
            w = ws[t][rr, cols].astype(F32)
            b = cin[s, rr].astype(F32)
            qs[t][rr, cols] = (w + LEAD * b).astype(BF16)
            uu, vv = squares(w, b)
            return acc[0] + fold(uu), acc[1] + fold(vv)

        return lax.fori_loop(0, F // STEP_D, inner, carry)

    def q_next(t, p):
        q_copy(t, p).start()

        @pl.when(p + 2 < NP)
        def _():
            load_b(t, p + 2, lax.rem(p, 2)).start()

    def choose(t, su, sv):
        lam = (jnp.sum(sv, keepdims=True) > jnp.sum(su, keepdims=True)).astype(F32)
        lam_l[t] = jnp.broadcast_to(lam, (8, 128))

    def q_rest(t, p, carry):
        carry = q_piece(t, p, carry)
        q_next(t, p)
        return carry

    zero = jnp.zeros((8, CH), F32)
    loads[2].wait()
    carry = q_piece(0, jnp.int32(0), (zero, zero))
    pl.semaphore_wait(bar, len(partners))
    for m in range(2):
        loads[m].wait()
        tok_start(m, 0, 5)
    q_next(0, jnp.int32(0))
    choose(0, *lax.fori_loop(1, NP, functools.partial(q_rest, 0), carry))
    for t in (1, 2):
        for s in range(2):
            load_b(t, s, s).start()
        loads[2 + t].wait()
        choose(t, *lax.fori_loop(0, NP, functools.partial(q_rest, t), (zero, zero)))
    lam_copy = remote(lam_l, lam_r, lam_s.at[0], lam_s.at[1], peer)
    lam_copy.start()

    def forward_near(m):
        tok_wait(m, zn_owner)
        tok_start(m, 5, 9)
        for i, d in enumerate((1, 2, 3)):
            tok_wait(m, y_owner[d])
            tok_start(m, 9 + i, 10 + i)

    def forward_far(m):
        for i, d in enumerate((1, 2, 3)):
            tok_wait(m, zy_owner[d])
            tok_start(m, 12 + i, 13 + i)

    def from_sibling(m):
        for i in range(8):
            tok_wait(m, 2 * i + 1 - k)

    forward_near(0)
    forward_near(1)
    forward_far(0)
    from_sibling(0)

    def rs_copy(t, src, d):
        return remote(src, rcv.at[t, d - 1], rs_s.at[t, d - 1], rs_r.at[t, d - 1], xdev(d))

    def partial_in(t, w_ref):
        def step(i, _):
            j = lax.rem(x + i + 1, 4)
            stg[t, i] = contract(xs[rows_of(j, CH)], w_ref[...], 1, 1)

            @pl.when(i < 3)
            def _():
                rs_copy(t, stg.at[t, i], i + 1).start()

            return 0

        lax.fori_loop(0, 4, step, 0)

    partial_in(0, wg)
    partial_in(1, wu)
    forward_far(1)
    from_sibling(1)

    for t in range(2):
        for d in (1, 2, 3):
            rs_copy(t, stg.at[t, d - 1], d).wait()

    def ag_copy(t, d, start=True):
        ref = (hid, dgt, dup)[t]
        rr = rows_of(x, CH)
        return remote(ref.at[rr], ref.at[rr], ag_s.at[t, d - 1], ag_r.at[t, d - 1], xdev(d))

    def ag_wait(t):
        ref = (hid, dgt, dup)[t]
        for d in (1, 2, 3):
            rr = rows_of(lax.rem(x + 4 - d, 4), CH)
            remote(ref.at[rr], ref.at[rr], ag_s.at[t, d - 1], ag_r.at[t, d - 1], xdev(d)).wait_recv()

    def make_hidden(i, _):
        rr = rows_of(i, STEP)
        gate = ((stg[0, 3, rr] + rcv[0, 0, rr]) + rcv[0, 1, rr]) + rcv[0, 2, rr]
        up = ((stg[1, 3, rr] + rcv[1, 0, rr]) + rcv[1, 1, rr]) + rcv[1, 2, rr]
        sig = jax.nn.sigmoid(gate)
        stg[0, 3, rr] = gate
        stg[1, 3, rr] = up
        hid[pl.ds(pl.multiple_of(x * CH + i * STEP, STEP), STEP)] = (gate * sig * up).astype(BF16)
        return 0

    lax.fori_loop(0, CH // STEP, make_hidden, 0)
    for d in (1, 2, 3):
        ag_copy(0, d).start()

    def partial_back(i, _):
        j = lax.rem(x + i + 1, 4)
        stg[0, i] = contract(gs[rows_of(j, CH)], wd[...], 1, 1)
        rs_copy(2, stg.at[0, i], i + 1).start()
        return 0

    lax.fori_loop(0, 3, partial_back, 0)
    own_b[...] = contract(gs[rows_of(x, CH)], wd[...], 1, 1)

    def p_copy(t, p):
        i = t * NP + p
        return remote(ws[t].at[:, rows_of(p, CH)], pr.at[i], p_s.at[i], p_r.at[i], peer)

    def step_matrix(t, left, right):
        for s in range(2):
            load_b(t, s, s).start()
        lam = lam_l[t, 0:1, 0:1]

        def piece(p, _):
            cols = rows_of(p, CH)
            s = lax.rem(p, 2)
            gt[...] = contract(left[...], right[:, cols], 0, 0)
            load_b(t, p, s).wait()

            def inner(i, _):
                rr = rows_of(i, STEP_D)
                w, b = ws[t][rr, cols].astype(F32), cin[s, rr].astype(F32)
                g = gt[rr] * (1.0 / TOK)
                new_b = 0.9 * b + 0.1 * g
                new_w = w - 0.5 * (0.3 * g + 0.7 * new_b)
                ws[t][rr, cols] = jnp.where(lam > 0.5, new_w, new_b).astype(BF16)
                return 0

            lax.fori_loop(0, F // STEP_D, inner, 0)
            p_copy(t, p).start()

            @pl.when(p + 2 < NP)
            def _():
                load_b(t, p + 2, s).start()

            return 0

        lax.fori_loop(0, NP, piece, 0)

    ag_wait(0)
    step_matrix(0, hid, gs)

    for d in (1, 2, 3):
        rs_copy(2, stg.at[0, d - 1], d).wait()

    def make_grads(i, _):
        rr = rows_of(i, STEP)
        back = ((own_b[rr] + rcv[2, 0, rr]) + rcv[2, 1, rr]) + rcv[2, 2, rr]
        gate, up = stg[0, 3, rr], stg[1, 3, rr]
        sig = jax.nn.sigmoid(gate)
        wr = pl.ds(pl.multiple_of(x * CH + i * STEP, STEP), STEP)
        dgt[wr] = (back * up * sig * (1.0 + gate * (1.0 - sig))).astype(BF16)
        dup[wr] = (back * (gate * sig)).astype(BF16)
        return 0

    lax.fori_loop(0, CH // STEP, make_grads, 0)
    for t in (1, 2):
        for d in (1, 2, 3):
            ag_copy(t, d).start()

    def token_part(grads, w_ref, first):
        def step(j, _):
            part = jnp.dot(grads[rows_of(j, CH)], w_ref[...], preferred_element_type=F32)
            part = part.reshape(2, 2, BLK, D)
            two = rows_of(j, 2)
            if first:
                tp[two] = part
            else:
                tp[two] = tp[two] + part
            return 0

        lax.fori_loop(0, 4, step, 0)

    ag_wait(1)
    token_part(dgt, wg, True)
    step_matrix(1, dgt, xs)
    ag_wait(2)
    token_part(dup, wu, False)
    tc_copy = remote(tp.at[:, 1 - k], tc, tc_s.at[0], tc_s.at[1], sib)
    tc_copy.start()
    step_matrix(2, dup, xs)

    lam_copy.wait()

    def means(t, q_a, p_a, q_b, p_b):
        la = rebuild(lam_l[t, 0:1, 0:1])
        lb = rebuild(lam_r[t, 0:1, 0:1])
        q_a, p_a, q_b, p_b = (v.astype(F32) for v in (q_a, p_a, q_b, p_b))
        w = (la[0] * q_a + la[1] * p_a) + (lb[0] * q_b + lb[1] * p_b)
        b = (la[2] * q_a + la[3] * p_a) + (lb[2] * q_b + lb[3] * p_b)
        return (0.5 * w).astype(BF16), (0.5 * b).astype(BF16)

    def load_q(t, p, s):
        return pltpu.make_async_copy(qr.at[t * NP + p], cin.at[s], cin_s.at[s])

    def combine(t):
        for s in range(2):
            q_copy(t, s).wait()
            load_q(t, s, s).start()

        def piece(p, _):
            s = lax.rem(p, 2)
            i = t * NP + p
            cols = rows_of(p, CH)
            load_q(t, p, s).wait()
            p_copy(t, p).wait()

            def inner(n, _):
                rr = rows_of(n, STEP_D)
                w, b = means(t, qs[t][rr, cols], ws[t][rr, cols], cin[s, rr], pr[i, rr])
                ws[t][rr, cols] = w
                qs[t][rr, cols] = b
                return 0

            lax.fori_loop(0, F // STEP_D, inner, 0)

            @pl.when(p + 2 < NP)
            def _():
                q_copy(t, p + 2).wait()
                load_q(t, p + 2, s).start()

            return 0

        lax.fori_loop(0, NP, piece, 0)

    tc_copy.wait()

    def add_core(i, _):
        tc[i] = tc[i] + tp[i, k]
        return 0

    lax.fori_loop(0, 8, add_core, 0)

    def ty_copy(d, half):
        to = half * 4 + lax.rem(y + d, 4)
        return remote(tc.at[to], ty.at[d - 1, half], ty_s.at[d - 1, half], ty_r.at[d - 1, half], ydev[d])

    for d in (1, 2, 3):
        for half in range(2):
            ty_copy(d, half).start()

    combine(0)

    for d in (1, 2, 3):
        for half in range(2):
            ty_copy(d, half).wait()

    def along_y(half):
        return ((tc[half * 4 + y] + ty[0, half]) + ty[1, half]) + ty[2, half]

    tzs[...] = along_y(1 - zl).astype(BF16)
    tz_copy = remote(tzs, tz, tz_s.at[0], tz_s.at[1], zn)
    tz_copy.start()

    combine(1)

    tz_copy.wait()
    tgo[...] = (along_y(zl) + tz[...].astype(F32)).astype(BF16)

    combine(2)

    for m in range(2):
        for owner, n, dev in sends[m]:
            tok(m, owner, n, dev).wait_send()
    for t in range(3):
        for d in (1, 2, 3):
            ag_copy(t, d).wait_send()


def body(tokens, grad_out, wg, wu, wd, bg, bu, bd):
    dma = pltpu.SemaphoreType.DMA
    whole = [(BLK, D)] + [(F, D)] * 6
    scratch = [
        pltpu.VMEM((TOK, D), BF16),
        pltpu.VMEM((TOK, D), BF16),
        pltpu.VMEM((3 * NP, F, CH), BF16),
        pltpu.VMEM((2, 4, CH, F), F32),
        pltpu.VMEM((CH, F), F32),
        pltpu.VMEM((3, 3, CH, F), F32),
        pltpu.VMEM((TOK, F), BF16),
        pltpu.VMEM((TOK, F), BF16),
        pltpu.VMEM((TOK, F), BF16),
        pltpu.VMEM((8, 2, BLK, D), F32),
        pltpu.VMEM((8, BLK, D), F32),
        pltpu.VMEM((3, 2, BLK, D), F32),
        pltpu.VMEM((BLK, D), BF16),
        pltpu.VMEM((BLK, D), BF16),
        pltpu.VMEM((F, CH), F32),
        pltpu.VMEM((2, F, CH), BF16),
        pltpu.VMEM((3, 8, 128), F32),
        pltpu.VMEM((3, 8, 128), F32),
        dma((5,)),
        dma((2,)),
        dma((2, 15)),
        dma((2, 16)),
        dma((3 * NP,)),
        dma((3 * NP,)),
        dma((3 * NP,)),
        dma((3 * NP,)),
        dma((2,)),
        dma((3, 3)),
        dma((3, 3)),
        dma((3, 3)),
        dma((3, 3)),
        dma((2,)),
        dma((3, 2)),
        dma((3, 2)),
        dma((2,)),
        dma((2,)),
    ]
    res = pl.pallas_call(
        kernel,
        out_shape=[pltpu.VMEM(s, BF16) for s in whole] + [jax.ShapeDtypeStruct((3 * NP, F, CH), BF16)],
        in_specs=[pl.BlockSpec(memory_space=pl.ANY)] * 8,
        out_specs=[pl.BlockSpec(memory_space=pltpu.VMEM)] * 7 + [pl.BlockSpec(memory_space=pl.ANY)],
        scratch_shapes=scratch,
        compiler_params=pltpu.CompilerParams(
            collective_id=0, has_side_effects=True, vmem_limit_bytes=48 * 2**20
        ),
        cost_estimate=pl.CostEstimate(
            flops=16 * TOK * D * F, bytes_accessed=40 * D * F, transcendentals=2 * CH * F
        ),
    )(tokens, grad_out, wg[0].T, wu[0].T, wd[0], bg[0].T, bu[0].T, bd[0])
    tg, gw, uw, dw, gb, ub, db = res[:7]
    return tg, gw.T, uw.T, dw, gb.T, ub.T, db


def solution(mesh):
    weights = (P("rep", "row", "col"), P("rep", "row", "col"), P("rep", "col", "row"))
    means = (P("row", "col"), P("row", "col"), P("col", "row"))
    return jax.shard_map(
        body,
        mesh=mesh,
        in_specs=(P(("rep", "col"), "row"),) * 2 + weights * 2,
        out_specs=(P(("rep", "col"), "row"),) + means * 2,
        check_vma=False,
    )
```

time: 360 us -> 322 us (0.89)
  local copies, waits for them, and re-layouts: 34.2 us -> 8.81 us
  Pallas kernels: 324 us -> 312 us
    unnamed x23 -> x7, local copies, waits for them, and re-layouts: 34.2 us -> 8.81 us
    pallas_call x1, Pallas kernels: 324 us -> 312 us  [body(): pl.pallas_call(kernel, out_shape=[pltpu.VMEM(s, BF16) for s in whole] + [...]
where the time goes in v2:
time: 322 us
  Pallas kernels  312 us (97%)
  local copies, waits for them, and re-layouts  8.81 us (3%)
    pallas_call x1, Pallas kernels, body(): pl.pallas_call(kernel, out_shape=[pltpu.VMEM(s, BF16) for s in whole] + [...  312 us
    unnamed x7, local copies, waits for them, and re-layouts  8.81 us

profile of v2, /device:TPU:0, one launch (start us, length us, event | category | flops | bytes accessed | tf_op | source)
XLA Modules:
  0.0 321.9 jit_solution(10822173567148752036)
XLA Ops:
  0.6 312.5 %shard_map.135 = (bf16[64,1280]{1,0:T(8,128)(2,1)S(1)}, bf16[864,1280]{1,0:T(8,128)(2,1)S(1)}, bf16[864,1280]{1,0:T(8,128)(2,1)S(1)}, bf16[864,1280]{1,0:T(8,128...) custom-call(bf16[64,1280]{1,0:T(8,128)(2,1)} %x_in.1, ...), custom_call_target="tpu_custom_call" | custom-call | flops 18119393280 | bytes 44236800 | tf_op jit(solution)/shard_map/pallas_call | solution.py:473
  313.1 0.7 copy.22
  313.8 1.4 copy.23
  315.2 1.4 copy.24
  316.5 1.4 copy.25
  317.9 1.4 copy.26
  319.2 1.4 copy.27
  320.6 1.4 copy.28

commit v3 on v2

--- a/solution.py
+++ b/solution.py
@@ -16,6 +16,8 @@
 BLK = 64
 CH = 256
 NP = D // CH
+PARTS = 3
+PART = F // PARTS
 STEP = 16
 STEP_D = 48
 MIX = 1.85
@@ -171,9 +173,10 @@
     loads[2].wait()
     carry = q_piece(0, jnp.int32(0), (zero, zero))
     pl.semaphore_wait(bar, len(partners))
-    for m in range(2):
-        loads[m].wait()
-        tok_start(m, 0, 5)
+    loads[0].wait()
+    tok_start(0, 0, 5)
+    loads[1].wait()
+    tok_start(1, 0, 1)
     q_next(0, jnp.int32(0))
     choose(0, *lax.fori_loop(1, NP, functools.partial(q_rest, 0), carry))
     for t in (1, 2):
@@ -201,7 +204,7 @@
             tok_wait(m, 2 * i + 1 - k)
 
     forward_near(0)
-    forward_near(1)
+    tok_start(1, 1, 5)
     forward_far(0)
     from_sibling(0)
 
@@ -222,6 +225,7 @@
         lax.fori_loop(0, 4, step, 0)
 
     partial_in(0, wg)
+    forward_near(1)
     partial_in(1, wu)
     forward_far(1)
     from_sibling(1)
@@ -264,9 +268,10 @@
     lax.fori_loop(0, 3, partial_back, 0)
     own_b[...] = contract(gs[rows_of(x, CH)], wd[...], 1, 1)
 
-    def p_copy(t, p):
+    def p_copy(t, p, h):
         i = t * NP + p
-        return remote(ws[t].at[:, rows_of(p, CH)], pr.at[i], p_s.at[i], p_r.at[i], peer)
+        rr = rows_of(h, PART)
+        return remote(ws[t].at[rr, rows_of(p, CH)], pr.at[i, rr], p_s.at[i, h], p_r.at[i, h], peer)
 
     def step_matrix(t, left, right):
         for s in range(2):
@@ -288,8 +293,12 @@
                 ws[t][rr, cols] = jnp.where(lam > 0.5, new_w, new_b).astype(BF16)
                 return 0
 
-            lax.fori_loop(0, F // STEP_D, inner, 0)
-            p_copy(t, p).start()
+            def part(h, _):
+                lax.fori_loop(h * (PART // STEP_D), (h + 1) * (PART // STEP_D), inner, 0)
+                p_copy(t, p, h).start()
+                return 0
+
+            lax.fori_loop(0, PARTS, part, 0)
 
             @pl.when(p + 2 < NP)
             def _():
@@ -365,7 +374,6 @@
             i = t * NP + p
             cols = rows_of(p, CH)
             load_q(t, p, s).wait()
-            p_copy(t, p).wait()
 
             def inner(n, _):
                 rr = rows_of(n, STEP_D)
@@ -374,7 +382,11 @@
                 qs[t][rr, cols] = b
                 return 0
 
-            lax.fori_loop(0, F // STEP_D, inner, 0)
+            def part(h, _):
+                p_copy(t, p, h).wait()
+                return lax.fori_loop(h * (PART // STEP_D), (h + 1) * (PART // STEP_D), inner, 0)
+
+            lax.fori_loop(0, PARTS, part, 0)
 
             @pl.when(p + 2 < NP)
             def _():
@@ -415,11 +427,10 @@
     tz_copy.start()
 
     combine(1)
+    combine(2)
 
     tz_copy.wait()
     tgo[...] = (along_y(zl) + tz[...].astype(F32)).astype(BF16)
-
-    combine(2)
 
     for m in range(2):
         for owner, n, dev in sends[m]:
@@ -427,6 +438,26 @@
     for t in range(3):
         for d in (1, 2, 3):
             ag_copy(t, d).wait_send()
+
+
+def flush_kernel(*refs):
+    n = len(refs) // 2
+    copies = [pltpu.make_async_copy(refs[i], refs[n + i], refs[-1].at[i]) for i in range(n)]
+    for cp in copies:
+        cp.start()
+    for cp in copies:
+        cp.wait()
+
+
+def flush(arrays):
+    return pl.pallas_call(
+        flush_kernel,
+        out_shape=[jax.ShapeDtypeStruct(a.shape, a.dtype) for a in arrays],
+        in_specs=[pl.BlockSpec(memory_space=pltpu.VMEM)] * len(arrays),
+        out_specs=[pl.BlockSpec(memory_space=pl.ANY)] * len(arrays),
+        scratch_shapes=[pltpu.SemaphoreType.DMA((len(arrays),))],
+        compiler_params=pltpu.CompilerParams(vmem_limit_bytes=2**20),
+    )(*[pltpu.with_memory_space_constraint(a, pltpu.VMEM) for a in arrays])
 
 
 def body(tokens, grad_out, wg, wu, wd, bg, bu, bd):
@@ -457,8 +488,8 @@
         dma((2, 16)),
         dma((3 * NP,)),
         dma((3 * NP,)),
-        dma((3 * NP,)),
-        dma((3 * NP,)),
+        dma((3 * NP, PARTS)),
+        dma((3 * NP, PARTS)),
         dma((2,)),
         dma((3, 3)),
         dma((3, 3)),
@@ -483,7 +514,7 @@
             flops=16 * TOK * D * F, bytes_accessed=40 * D * F, transcendentals=2 * CH * F
         ),
     )(tokens, grad_out, wg[0].T, wu[0].T, wd[0], bg[0].T, bu[0].T, bd[0])
-    tg, gw, uw, dw, gb, ub, db = res[:7]
+    tg, gw, uw, dw, gb, ub, db = flush(res[:7])
     return tg, gw.T, uw.T, dw, gb.T, ub.T, db
 
 

time: 322 us -> 310 us (0.963)
  local copies, waits for them, and re-layouts: 8.81 us -> 0 us
    unnamed x7 -> x0, local copies, waits for them, and re-layouts: 8.81 us -> none
    pallas_call x1, Pallas kernels: 312 us -> 304 us  [body(): pl.pallas_call(kernel, out_shape=[pltpu.VMEM(s, BF16) for s in whole] + [...]
    pallas_call x0 -> x1, Pallas kernels: none -> 4.93 us  [flush(): pl.pallas_call(flush_kernel, out_shape=[jax.ShapeDtypeStruct(a.shape, a.d...]
where the time goes in v3:
time: 310 us
  Pallas kernels  309 us (100%)
    pallas_call x1, Pallas kernels, body(): pl.pallas_call(kernel, out_shape=[pltpu.VMEM(s, BF16) for s in whole] + [...  304 us

profile of v3, /device:TPU:0, one launch (start us, length us, event | category | flops | bytes accessed | tf_op | source)
XLA Modules:
  0.0 309.5 jit_solution(5404955942259725386)
XLA Ops:
  0.6 304.0 %shard_map.135 = (bf16[64,1280]{1,0:T(8,128)(2,1)S(1)}, bf16[864,1280]{1,0:T(8,128)(2,1)S(1)}, bf16[864,1280]{1,0:T(8,128)(2,1)S(1)}, bf16[864,1280]{1,0:T(8,128...) custom-call(bf16[64,1280]{1,0:T(8,128)(2,1)} %x_in.1, ...), custom_call_target="tpu_custom_call" | custom-call | flops 18119393280 | bytes 44236800 | tf_op jit(solution)/shard_map/pallas_call | solution.py:504
  304.6 4.9 %shard_map.136 = (bf16[64,1280]{1,0:T(8,128)(2,1)}, bf16[864,1280]{1,0:T(8,128)(2,1)}, bf16[864,1280]{1,0:T(8,128)(2,1)}, bf16[864,1280]{1,0:T(8,128)(2,1)}, bf1...) custom-call(bf16[64,1280]{1,0:T(8,128)(2,1)S(1)} %get-tuple-element.21.refs_0_, ...), custom_call_target="tpu_custom_call" | custom-call | tf_op jit(solution)/shard_map/pallas_call | solution.py:453

commit v4 on v3

--- a/solution.py
+++ b/solution.py
@@ -427,17 +427,20 @@
     tz_copy.start()
 
     combine(1)
-    combine(2)
-
-    tz_copy.wait()
-    tgo[...] = (along_y(zl) + tz[...].astype(F32)).astype(BF16)
-
+
+    mine = zl * 4 + y
+    tc[mine] = along_y(zl)
     for m in range(2):
         for owner, n, dev in sends[m]:
             tok(m, owner, n, dev).wait_send()
     for t in range(3):
         for d in (1, 2, 3):
             ag_copy(t, d).wait_send()
+
+    combine(2)
+
+    tz_copy.wait()
+    tgo[...] = (tc[mine] + tz[...].astype(F32)).astype(BF16)
 
 
 def flush_kernel(*refs):

time: 310 us -> 310 us (level)
  no operation moved by 1% of the time
where the time goes in v4:
time: 310 us; the launch traced here: 309 us
  Pallas kernels  309 us (100%)
    pallas_call x1, Pallas kernels, body(): pl.pallas_call(kernel, out_shape=[pltpu.VMEM(s, BF16) for s in whole] + [...  304 us

profile of v4, /device:TPU:0, one launch (start us, length us, event | category | flops | bytes accessed | tf_op | source)
XLA Modules:
  0.0 309.4 jit_solution(7589605472779894995)
XLA Ops:
  0.6 303.9 %shard_map.135 = (bf16[64,1280]{1,0:T(8,128)(2,1)S(1)}, bf16[864,1280]{1,0:T(8,128)(2,1)S(1)}, bf16[864,1280]{1,0:T(8,128)(2,1)S(1)}, bf16[864,1280]{1,0:T(8,128...) custom-call(bf16[64,1280]{1,0:T(8,128)(2,1)} %x_in.1, ...), custom_call_target="tpu_custom_call" | custom-call | flops 18119393280 | bytes 44236800 | tf_op jit(solution)/shard_map/pallas_call | solution.py:507
  304.5 4.9 %shard_map.136 = (bf16[64,1280]{1,0:T(8,128)(2,1)}, bf16[864,1280]{1,0:T(8,128)(2,1)}, bf16[864,1280]{1,0:T(8,128)(2,1)}, bf16[864,1280]{1,0:T(8,128)(2,1)}, bf1...) custom-call(bf16[64,1280]{1,0:T(8,128)(2,1)S(1)} %get-tuple-element.21.refs_0_, ...), custom_call_target="tpu_custom_call" | custom-call | tf_op jit(solution)/shard_map/pallas_call | solution.py:456

commit v5 on v4

--- a/solution.py
+++ b/solution.py
@@ -81,8 +81,7 @@
         load(wg_in, wg, 3),
         load(wu_in, wu, 4),
     ]
-    for cp in loads:
-        cp.start()
+    loads[2].start()
 
     bs = (bd_in, bg_in, bu_in)
 
@@ -91,6 +90,8 @@
 
     for s in range(2):
         load_b(0, s, s).start()
+    for i in (0, 1, 3, 4):
+        loads[i].start()
 
     def remote(src, dst, ss, rs, dev):
         return pltpu.make_async_remote_copy(
@@ -101,7 +102,8 @@
 
     def tok(m, owner, n, dev):
         blk = mats[m].at[rows_of(owner, BLK)]
-        return remote(blk, blk, tok_s.at[m, n], tok_r.at[m, owner], dev)
+        src = (x_in, g_in)[m] if n < 5 else blk
+        return remote(src, blk, tok_s.at[m, n], tok_r.at[m, owner], dev)
 
     zn_owner = col_of(1 - zl, y, k)
     y_owner = {d: col_of(zl, lax.rem(y + 4 - d, 4), k) for d in (1, 2, 3)}
@@ -170,18 +172,14 @@
         return carry
 
     zero = jnp.zeros((8, CH), F32)
-    loads[2].wait()
-    carry = q_piece(0, jnp.int32(0), (zero, zero))
     pl.semaphore_wait(bar, len(partners))
-    loads[0].wait()
-    tok_start(0, 0, 5)
-    loads[1].wait()
-    tok_start(1, 0, 1)
-    q_next(0, jnp.int32(0))
-    choose(0, *lax.fori_loop(1, NP, functools.partial(q_rest, 0), carry))
-    for t in (1, 2):
-        for s in range(2):
-            load_b(t, s, s).start()
+    for m in range(2):
+        tok_start(m, 0, 1)
+    tok_start(0, 1, 5)
+    for t in range(3):
+        if t:
+            for s in range(2):
+                load_b(t, s, s).start()
         loads[2 + t].wait()
         choose(t, *lax.fori_loop(0, NP, functools.partial(q_rest, t), (zero, zero)))
     lam_copy = remote(lam_l, lam_r, lam_s.at[0], lam_s.at[1], peer)
@@ -207,6 +205,7 @@
     tok_start(1, 1, 5)
     forward_far(0)
     from_sibling(0)
+    loads[0].wait()
 
     def rs_copy(t, src, d):
         return remote(src, rcv.at[t, d - 1], rs_s.at[t, d - 1], rs_r.at[t, d - 1], xdev(d))
@@ -229,6 +228,7 @@
     partial_in(1, wu)
     forward_far(1)
     from_sibling(1)
+    loads[1].wait()
 
     for t in range(2):
         for d in (1, 2, 3):
@@ -445,7 +445,12 @@
 
 def flush_kernel(*refs):
     n = len(refs) // 2
-    copies = [pltpu.make_async_copy(refs[i], refs[n + i], refs[-1].at[i]) for i in range(n)]
+    copies = []
+    for i in range(n):
+        parts = 1 if refs[i].shape[0] < F else PARTS
+        for h in range(parts):
+            rr = pl.ds(h * (refs[i].shape[0] // parts), refs[i].shape[0] // parts)
+            copies.append(pltpu.make_async_copy(refs[i].at[rr], refs[n + i].at[rr], refs[-1].at[i, h]))
     for cp in copies:
         cp.start()
     for cp in copies:
@@ -458,7 +463,7 @@
         out_shape=[jax.ShapeDtypeStruct(a.shape, a.dtype) for a in arrays],
         in_specs=[pl.BlockSpec(memory_space=pltpu.VMEM)] * len(arrays),
         out_specs=[pl.BlockSpec(memory_space=pl.ANY)] * len(arrays),
-        scratch_shapes=[pltpu.SemaphoreType.DMA((len(arrays),))],
+        scratch_shapes=[pltpu.SemaphoreType.DMA((len(arrays), PARTS))],
         compiler_params=pltpu.CompilerParams(vmem_limit_bytes=2**20),
     )(*[pltpu.with_memory_space_constraint(a, pltpu.VMEM) for a in arrays])
 

time: 310 us -> 310 us (level)
  no operation moved by 1% of the time
where the time goes in v5:
time: 310 us
  Pallas kernels  309 us (100%)
    pallas_call x1, Pallas kernels, body(): pl.pallas_call(kernel, out_shape=[pltpu.VMEM(s, BF16) for s in whole] + [...  304 us

profile of v5, /device:TPU:0, one launch (start us, length us, event | category | flops | bytes accessed | tf_op | source)
XLA Modules:
  0.0 309.5 jit_solution(7913146306691718840)
XLA Ops:
  0.6 303.9 %shard_map.135 = (bf16[64,1280]{1,0:T(8,128)(2,1)S(1)}, bf16[864,1280]{1,0:T(8,128)(2,1)S(1)}, bf16[864,1280]{1,0:T(8,128)(2,1)S(1)}, bf16[864,1280]{1,0:T(8,128...) custom-call(bf16[64,1280]{1,0:T(8,128)(2,1)} %x_in.1, ...), custom_call_target="tpu_custom_call" | custom-call | flops 18119393280 | bytes 44236800 | tf_op jit(solution)/shard_map/pallas_call | solution.py:512
  304.5 5.0 %shard_map.136 = (bf16[64,1280]{1,0:T(8,128)(2,1)}, bf16[864,1280]{1,0:T(8,128)(2,1)}, bf16[864,1280]{1,0:T(8,128)(2,1)}, bf16[864,1280]{1,0:T(8,128)(2,1)}, bf1...) custom-call(bf16[64,1280]{1,0:T(8,128)(2,1)S(1)} %get-tuple-element.21.refs_0_, ...), custom_call_target="tpu_custom_call" | custom-call | tf_op jit(solution)/shard_map/pallas_call | solution.py:461
